TPU v7x, 256 devices: a whole 4x4x8 slice. The times are simulated.
256 devices in a mesh: seq: 64 (over z, y, core), dp: 4 (over x).
Axes of the slice: x: 4, y: 4, z: 8, core: 2. Of those that a mesh axis runs over, the one named last changes fastest.
Arguments:
- queries: bfloat16 [4, 32768, 1024], P('dp', 'seq'), may hold values from -8 to 8
- memory_keys: bfloat16 [4, 32768, 1024], P('dp', 'seq'), may hold values from -8 to 8
- memory_values: bfloat16 [4, 32768, 1024], P('dp', 'seq'), may hold values from -6 to 6
- out_weight: bfloat16 [1024, 2048], P('seq'), may hold values from -0.1875 to 0.1875
- grad_out: bfloat16 [4, 32768, 2048], P('dp', 'seq'), may hold values from -6 to 6
- key_first: int32 [4, 256], P('dp', 'seq'), may hold values from 0 to 254, as said below
- key_last: int32 [4, 256], P('dp', 'seq'), may hold values from 2 to 256
Outputs:
- layer_out: bfloat16 [4, 32768, 2048], P('dp', 'seq')
- grad_query: bfloat16 [4, 32768, 1024], P('dp', 'seq')
- grad_keys: bfloat16 [4, 32768, 1024], P('dp', 'seq')
- grad_values: bfloat16 [4, 32768, 1024], P('dp', 'seq')
- weight_grad: float32 [1024, 2048], P('seq')
Inputs may be any that keep to these rules, and one draw needn't show every extreme that they name: With key_last: query block b of pack p attends to key blocks key_first[p, b] to key_last[p, b] - 1, blocks of 128 tokens. Sentence pairs tile aligned groups of 4 blocks that begin at block 2, the first and last groups holding 4 // 2 blocks; a query block's key blocks lie in its own group and number 1 to 3, 3 in some group of every pack.
All inputs are finite; a program needn't handle non-finite values.
Results may differ from a plain program's by a relative error of at most 0.0095.
Values may be sent and summed in bfloat16 or wider, within the bound.
A program may use at most 192 MiB of HBM per device.

v0:
```python
import math
import jax
import jax.numpy as jnp
from jax import lax
from jax.sharding import PartitionSpec as P

HDIM = 128
HEADS = 8
BLOCK = 128
REACH = 256


def padded_2(block, sides, width):
    for axis, dim in sides:
        count = lax.axis_size(axis)
        forward = [(i, i + 1) for i in range(count - 1)]
        backward = [(target, source) for source, target in forward]
        low = lax.ppermute(
            lax.slice_in_dim(block, block.shape[dim] - width, None, axis=dim), axis, forward
        )
        high = lax.ppermute(lax.slice_in_dim(block, 0, width, axis=dim), axis, backward)
        block = jnp.concatenate([low, block, high], axis=dim)
    return block


def passed_along(block, axis, distance):
    devices = range(lax.axis_size(axis))
    route = [(i - distance, i) for i in devices if i - distance in devices]
    return lax.ppermute(block, axis, route)


def run_tiles(
    query_rows, grad_rows, kv_source, window_starts, window_rows, lower, upper, row_anchor
):
    rows_dev, width_hd = query_rows.shape
    set_count = rows_dev // BLOCK // 4
    score_scale = 1.0 / math.sqrt(HDIM)

    def advance(running, set_index):
        member_ids = set_index * 4 + jnp.arange(4, dtype=jnp.int32)
        query_set = query_rows.reshape(4, BLOCK, HEADS, HDIM)
        grad_set = grad_rows.reshape(4, BLOCK, HEADS, HDIM)
        starts = window_starts[member_ids]
        kv_tiles = jax.vmap(
            lambda offset: lax.dynamic_slice_in_dim(kv_source, offset, window_rows, 1)
        )(starts)
        key_tiles = kv_tiles[:, 0].reshape(4, window_rows, HEADS, HDIM)
        value_tiles = kv_tiles[:, 1].reshape(4, window_rows, HEADS, HDIM)
        positions = (
            row_anchor + starts[:, None] + jnp.arange(window_rows, dtype=jnp.int32)[None, :]
        ) // BLOCK
        allowed = (positions >= lower[member_ids][:, None]) & (
            positions < upper[member_ids][:, None]
        )
        inside = allowed[:, None, None, :]
        scores = (
            jnp.einsum("jqhd,jkhd->jhqk", query_set, key_tiles, preferred_element_type=jnp.float32)
            * score_scale
        )
        highest = jnp.max(jnp.where(inside, scores, -jnp.inf), axis=-1, keepdims=True)
        raised = jnp.where(inside, jnp.exp(scores - highest), 0.0)
        softmax_probs = raised / jnp.sum(raised, axis=-1, keepdims=True)
        weights = softmax_probs.astype(jnp.bfloat16)
        attended = jnp.einsum(
            "jhqk,jkhd->jqhd", weights, value_tiles, preferred_element_type=jnp.float32
        ).astype(jnp.bfloat16)
        grad_probs = jnp.einsum(
            "jqhd,jkhd->jhqk", grad_set, value_tiles, preferred_element_type=jnp.float32
        )
        row_term = jnp.sum(softmax_probs * grad_probs, axis=-1, keepdims=True)
        grad_scores = (softmax_probs * (grad_probs - row_term) * score_scale).astype(jnp.bfloat16)
        grad_query = jnp.einsum(
            "jhqk,jkhd->jqhd", grad_scores, key_tiles, preferred_element_type=jnp.float32
        ).astype(jnp.bfloat16)
        key_part = jnp.einsum(
            "jhqk,jqhd->jkhd", grad_scores, query_set, preferred_element_type=jnp.float32
        ).reshape(4, window_rows, width_hd)
        value_part = jnp.einsum(
            "jhqk,jqhd->jkhd", weights, grad_set, preferred_element_type=jnp.float32
        ).reshape(4, window_rows, width_hd)
        contributions = jnp.stack([key_part, value_part], axis=1)
        for member in range(4):
            offset = starts[member]
            current = lax.dynamic_slice_in_dim(running, offset, window_rows, 1)
            running = lax.dynamic_update_slice_in_dim(
                running, current + contributions[member], offset, 1
            )
        return (
            running,
            (attended.reshape(4 * BLOCK, width_hd), grad_query.reshape(4 * BLOCK, width_hd)),
        )

    empty_sum = jnp.zeros((2, kv_source.shape[1], width_hd), jnp.float32)
    grad_sums, outputs = lax.scan(advance, empty_sum, jnp.arange(set_count, dtype=jnp.int32))
    return (
        grad_sums,
        outputs[0].reshape(rows_dev, width_hd),
        outputs[1].reshape(rows_dev, width_hd),
    )


def body(queries, memory_keys, memory_values, out_weight, grad_out, key_first, key_last):
    query_rows = queries[0]
    dy_rows = grad_out[0]
    first_blocks = key_first[0]
    last_blocks = key_last[0]
    rows_dev, width_hd = query_rows.shape
    block_count = rows_dev // BLOCK
    window_rows = BLOCK + 2 * REACH
    whole_weight = lax.all_gather(out_weight, "seq", axis=0, tiled=True)
    grad_attn = lax.dot_general(
        dy_rows, whole_weight, (((1,), (1,)), ((), ())), preferred_element_type=jnp.float32
    ).astype(jnp.bfloat16)
    stacked = jnp.stack([memory_keys[0], memory_values[0]])
    padded = padded_2(stacked, (("seq", 1),), REACH)
    halo_anchor = lax.axis_index("seq") * rows_dev - REACH
    window_starts = jnp.arange(block_count, dtype=jnp.int32) * BLOCK
    grad_sums, attended, grad_query = run_tiles(
        query_rows,
        grad_attn,
        padded,
        window_starts,
        window_rows,
        first_blocks,
        last_blocks,
        halo_anchor,
    )
    left_rim = grad_sums[:, :REACH]
    right_rim = grad_sums[:, REACH + rows_dev :]
    from_right = passed_along(left_rim.astype(jnp.bfloat16), "seq", -1).astype(left_rim.dtype)
    from_left = passed_along(right_rim.astype(jnp.bfloat16), "seq", 1).astype(right_rim.dtype)
    own_sums = grad_sums[:, REACH : REACH + rows_dev]
    own_sums = own_sums.at[:, :REACH].add(from_left)
    own_sums = own_sums.at[:, rows_dev - REACH :].add(from_right)
    key_grad = own_sums[0].astype(jnp.bfloat16)
    value_grad = own_sums[1].astype(jnp.bfloat16)
    layer_out = jnp.dot(attended, whole_weight, preferred_element_type=jnp.float32).astype(
        jnp.bfloat16
    )
    normalizer = math.sqrt(lax.axis_size("seq") * rows_dev)
    shard_sum = lax.psum_scatter(
        lax.dot_general(
            attended, dy_rows, (((0,), (0,)), ((), ())), preferred_element_type=jnp.float32
        ),
        "seq",
        scatter_dimension=0,
        tiled=True,
    )
    summed = lax.psum(shard_sum.astype(jnp.bfloat16), "dp").astype(jnp.float32)
    weight_grad = summed / normalizer
    return (layer_out[None], grad_query[None], key_grad[None], value_grad[None], weight_grad)


def solution(mesh):
    return jax.shard_map(
        body,
        mesh=mesh,
        in_specs=(
            P("dp", "seq", None),
            P("dp", "seq", None),
            P("dp", "seq", None),
            P("seq", None),
            P("dp", "seq", None),
            P("dp", "seq"),
            P("dp", "seq"),
        ),
        out_specs=(
            P("dp", "seq", None),
            P("dp", "seq", None),
            P("dp", "seq", None),
            P("dp", "seq", None),
            P("seq", None),
        ),
        check_vma=False,
    )
```

profile of v0, /device:TPU:8, one launch (start us, length us, event | category | flops | bytes accessed | tf_op | source)
XLA Modules:
  0.0 405.0 jit_solution(8110936625988158264)
XLA Ops:
  22.9 5.4 %collective-permute-done.1 = bf16[2,256,1024]{2,1,0:T(8,128)(2,1)} collective-permute-done((bf16[2,256,1024]{2,1,0:T(8,128)(2,1)}, bf16[2,256,1024]{2,1,0:T(8,128)(2,1)}, u32[]{:S(2)}, u32[]{:S(2)}) %collective-permute-start.1) | collective-permute-done | bytes 1048608 | tf_op jit(solution)/shard_map/ppermute | solution.py:21
  36.5 21.0 %while.3 = (s32[]{:T(128)}, bf16[2,1024,1024]{2,1,0:T(8,128)(2,1)}, s32[4,3]{1,0:T(4,128)S(1)}, bf16[4,2,640,1024]{3,2,1,0:T(8,128)(2,1)}, s32[]{:T(128)}) while((s32[]{:T(128)}, bf16[2,1024,1024]{2,1,0:T(8,128)(2,1)}, s32[4,3]{1,0:T(4,128)S(1)}, bf16[4,2,640,1024]{3,2,1,0:T(8,128)(2,1)}, s32[]{:T(128)}) %tuple.39), condition=%wide.while_cond.2, body=%wide.while_body.2.sunk | while | flops 2 | bytes 5243501 | solution.py:45
  57.4 5.4 %slice.116 = bf16[4,1,640,1024]{3,2,1,0:T(8,128)(2,1)} slice(bf16[4,2,640,1024]{3,2,1,0:T(8,128)(2,1)} %get-tuple-element.69), slice={[0:4], [1:2], [0:640], [0:1024]} | slice | bytes 10485760 | tf_op jit(solution)/shard_map/while/body/eval_jaxpr/slice | solution.py:48
  62.9 15.4 %copy.30 = bf16[4,2,640,1024]{2,3,0,1:T(8,128)(2,1)} copy(bf16[4,2,640,1024]{3,2,1,0:T(8,128)(2,1)} %get-tuple-element.69) | data formatting | bytes 20971520 | tf_op jit(solution)/shard_map/while/body/eval_jaxpr/vmap()/gather | solution.py:45
  78.2 8.0 %copy.29 = bf16[4,1,640,1024]{2,3,0,1:T(8,128)(2,1)} copy(bf16[4,1,640,1024]{3,2,1,0:T(8,128)(2,1)} %slice.116) | data formatting | bytes 10485760 | tf_op jit(solution)/shard_map/while/body/eval_jaxpr/slice | solution.py:48
  91.6 14.1 %bitcast_reduce_fusion = (f32[4,8,128]{2,1,0:T(8,128)S(1)}, f32[4,8,640,128]{3,2,1,0:T(8,128)}) fusion(pred[4,640]{1,0:T(4,128)(4,1)S(1)} %compare_and_fusion, bf16[4,640,8,128]{1,3,2,0:T(8,128)(2,1)} %bitcast.112, bf16[4,128,8,128]{1,3,2,0:T(8,128)(2,1)S(1)} %copy-done.6), kind=kOutput, calls=%fused_computation.14 | convolution fusion | flops 1357906560 | bytes 16796160 | tf_op jit(solution)/shard_map/while/body/eval_jaxpr/sub | solution.py:61
  105.7 8.1 %fusion.50 = bf16[4,128,8,128]{1,3,2,0:T(8,128)(2,1)} fusion(bf16[4,640,8,128]{1,3,2,0:T(8,128)(2,1)} %bitcast.108, f32[4,8,640,128]{3,2,1,0:T(8,128)} %get-tuple-element.97, f32[4,8,128]{2,1,0:T(8,128)S(1)} %get-tuple-element.96), kind=kOutput, calls=%fused_computation.58 | convolution fusion | flops 676855808 | bytes 16793600 | tf_op jit(solution)/shard_map/while/body/eval_jaxpr/jhqk,jkhd->jqhd/dot_general | solution.py:64
  116.2 7.0 %fusion.37 = f32[1024,2048]{1,0:T(8,128)} fusion(bf16[1,512,2048]{2,1,0:T(8,128)(2,1)S(1)} %copy-done, bf16[64,8,8,128]{3,2,1,0:T(8,128)(2,1)} %bitcast.117), kind=kOutput, calls=%fused_computation.51 | convolution fusion | flops 2147483648 | bytes 11534336 | tf_op jit(solution)/shard_map/dot_general | solution.py:142
  137.4 7.9 %fusion.78 = f32[4,8,128,640]{2,3,1,0:T(8,128)} fusion(bf16[4,128,8,128]{1,3,2,0:T(8,128)(2,1)S(1)} %copy.43, bf16[4,640,8,128]{1,3,2,0:T(8,128)(2,1)} %bitcast.109), kind=kOutput, calls=%fused_computation.94 | convolution fusion | flops 671088640 | bytes 16777216 | tf_op jit(solution)/shard_map/while/body/eval_jaxpr/jqhd,jkhd->jhqk/dot_general | solution.py:67
  145.3 18.9 %fusion.10 = f32[4,8,640,128]{2,3,1,0:T(8,128)} fusion(bf16[4,128,8,128]{1,3,2,0:T(8,128)(2,1)S(1)} %copy-done.6, f32[4,8,128,640]{2,3,1,0:T(8,128)} %fusion.78, f32[4,8,640,128]{3,2,1,0:T(8,128)} %get-tuple-element.97, f32[4,8,128]{2,1,0:T(8,128)S(1)} %get-tuple-element.96), kind=kOutput, calls=%fused_computation.22 | convolution fusion | flops 689443456 | bytes 32522240 | tf_op jit(solution)/shard_map/while/body/eval_jaxpr/jhqk,jqhd->jkhd/dot_general | solution.py:75
  164.2 11.4 %copy.45 = f32[4,1,640,1024]{3,2,1,0:T(8,128)} copy(f32[4,1,640,1024]{2,3,0,1:T(8,128)} %bitcast.110) | data formatting | bytes 20971520 | tf_op jit(solution)/shard_map/while/body/eval_jaxpr/stack;while/body/eval_jaxpr/reshape | solution.py:81
  175.6 10.2 %fusion.31 = f32[4,8,128,640]{3,2,1,0:T(8,128)} fusion(bf16[4,128,8,128]{1,3,2,0:T(8,128)(2,1)S(1)} %copy.43, f32[4,8,640,128]{3,2,1,0:T(8,128)} %get-tuple-element.97, f32[4,8,128]{2,1,0:T(8,128)S(1)} %get-tuple-element.96), kind=kOutput, calls=%fused_computation.43 | convolution fusion | flops 676331520 | bytes 22036480 | tf_op jit(solution)/shard_map/while/body/eval_jaxpr/jhqk,jqhd->jkhd/dot_general | solution.py:78
  185.8 11.4 %copy.46 = f32[4,1,640,1024]{3,2,1,0:T(8,128)} copy(f32[4,1,640,1024]{2,3,0,1:T(8,128)} %bitcast.111) | data formatting | bytes 20971520 | tf_op jit(solution)/shard_map/while/body/eval_jaxpr/stack;while/body/eval_jaxpr/reshape | solution.py:81
  197.2 5.7 %fusion.19 = f32[2,640,1024]{2,1,0:T(8,128)} fusion(f32[4,1,640,1024]{3,2,1,0:T(8,128)} %copy.45, f32[4,1,640,1024]{3,2,1,0:T(8,128)} %copy.46), kind=kLoop, calls=%fused_computation.28 | loop fusion | flops 1310720 | bytes 26214400 | tf_op jit(solution)/shard_map/while/body/eval_jaxpr/squeeze | solution.py:86
  207.2 15.0 %dynamic_update_slice.21 = f32[2,1024,1024]{2,1,0:T(8,128)} dynamic-update-slice(f32[2,1024,1024]{2,1,0:T(8,128)} %broadcast_in_dim.65, f32[2,640,1024]{2,1,0:T(8,128)} %fusion.19, s32[]{:T(128)} %constant.105.clone.1, s32[]{:T(128)S(6)} %select_n.64, s32[]{:T(128)} %constant.105.clone.1) | dynamic-update-slice | bytes 10485764 | tf_op jit(solution)/shard_map/while/body/eval_jaxpr/dynamic_update_slice | solution.py:85
  222.2 8.5 %fusion.22 = f32[2,640,1024]{2,1,0:T(8,128)} fusion(f32[4,1,640,1024]{3,2,1,0:T(8,128)} %copy.45, f32[4,1,640,1024]{3,2,1,0:T(8,128)} %copy.46, f32[2,1024,1024]{2,1,0:T(8,128)} %dynamic_update_slice.21, s32[]{:T(128)S(6)} %select_n.65), kind=kLoop, calls=%fused_computation.31 | loop fusion | flops 2621440 | bytes 31457284 | tf_op jit(solution)/shard_map/while/body/eval_jaxpr/add | solution.py:86
  230.7 15.0 %dynamic_update_slice.22 = f32[2,1024,1024]{2,1,0:T(8,128)} dynamic-update-slice(f32[2,1024,1024]{2,1,0:T(8,128)} %dynamic_update_slice.21, f32[2,640,1024]{2,1,0:T(8,128)} %fusion.22, s32[]{:T(128)} %constant.105.clone.1, s32[]{:T(128)S(6)} %select_n.65, s32[]{:T(128)} %constant.105.clone.1) | dynamic-update-slice | bytes 10485764 | tf_op jit(solution)/shard_map/while/body/eval_jaxpr/dynamic_update_slice | solution.py:85
  245.6 8.3 %fusion.17 = f32[2,640,1024]{2,1,0:T(8,128)} fusion(f32[4,1,640,1024]{3,2,1,0:T(8,128)} %copy.45, f32[4,1,640,1024]{3,2,1,0:T(8,128)} %copy.46, f32[2,1024,1024]{2,1,0:T(8,128)} %dynamic_update_slice.22, s32[]{:T(128)S(6)} %select_n.66), kind=kLoop, calls=%fused_computation.26 | loop fusion | flops 2621440 | bytes 31457284 | tf_op jit(solution)/shard_map/while/body/eval_jaxpr/add | solution.py:86
  253.9 14.9 %dynamic_update_slice.23 = f32[2,1024,1024]{2,1,0:T(8,128)} dynamic-update-slice(f32[2,1024,1024]{2,1,0:T(8,128)} %dynamic_update_slice.22, f32[2,640,1024]{2,1,0:T(8,128)} %fusion.17, s32[]{:T(128)} %constant.105.clone.1, s32[]{:T(128)S(6)} %select_n.66, s32[]{:T(128)} %constant.105.clone.1) | dynamic-update-slice | bytes 10485764 | tf_op jit(solution)/shard_map/while/body/eval_jaxpr/dynamic_update_slice | solution.py:85
  268.8 8.3 %fusion.24 = f32[2,640,1024]{2,1,0:T(8,128)} fusion(f32[4,1,640,1024]{3,2,1,0:T(8,128)} %copy.46, f32[4,1,640,1024]{3,2,1,0:T(8,128)} %copy.45, f32[2,1024,1024]{2,1,0:T(8,128)} %dynamic_update_slice.23, s32[]{:T(128)S(6)} %select_n.67), kind=kLoop, calls=%fused_computation.34 | loop fusion | flops 2621440 | bytes 31457284 | tf_op jit(solution)/shard_map/while/body/eval_jaxpr/add | solution.py:86
  277.0 14.3 %dynamic_update_slice.24 = f32[2,1024,1024]{2,1,0:T(8,128)} dynamic-update-slice(f32[2,1024,1024]{2,1,0:T(8,128)} %dynamic_update_slice.23, f32[2,640,1024]{2,1,0:T(8,128)} %fusion.24, s32[]{:T(128)} %constant.105.clone.1, s32[]{:T(128)S(6)} %select_n.67, s32[]{:T(128)} %constant.105.clone.1) | dynamic-update-slice | bytes 10485764 | tf_op jit(solution)/shard_map/while/body/eval_jaxpr/dynamic_update_slice | solution.py:85
  302.5 19.4 %fusion.53 = bf16[4,128,8,128]{1,3,2,0:T(8,128)(2,1)} fusion(bf16[4,640,8,128]{1,3,2,0:T(8,128)(2,1)} %bitcast.113, f32[4,8,128,640]{2,3,1,0:T(8,128)} %fusion.78, f32[4,8,640,128]{3,2,1,0:T(8,128)} %get-tuple-element.97, f32[4,8,128]{2,1,0:T(8,128)S(1)} %get-tuple-element.96), kind=kOutput, calls=%fused_computation.59 | convolution fusion | flops 689967744 | bytes 27279360 | tf_op jit(solution)/shard_map/while/body/eval_jaxpr/jhqk,jkhd->jqhd/dot_general | solution.py:72
  329.8 6.0 %fusion.30 = bf16[1,512,2048]{2,1,0:T(8,128)(2,1)} fusion(bf16[1024,2048]{1,0:T(8,128)(2,1)} %all-gather.2.cloned.1.call-done, bf16[64,8,8,128]{3,2,1,0:T(8,128)(2,1)S(1)} %bitcast.118), kind=kOutput, calls=%fused_computation.42 | convolution fusion | flops 2148532224 | bytes 7340032 | tf_op jit(solution)/shard_map/dot_general | solution.py:137
  345.0 51.9 %all-reduce.2.cloned.1.call-done = bf16[16,2048]{1,0:T(8,128)(2,1)} async-done(((bf16[16,2048]{1,0:T(8,128)(2,1)}), bf16[16,2048]{1,0:T(8,128)(2,1)}) %all-reduce.2.cloned.1.call-update) | async-done | bytes 65552 | tf_op jit(solution)/shard_map/psum | solution.py:149
  (80 shorter events, 92.9 us)
Async XLA Ops:
  7.2 109.0 %copy-start = (bf16[1,512,2048]{2,1,0:T(8,128)(2,1)S(1)}, bf16[1,512,2048]{2,1,0:T(8,128)(2,1)}, u32[]{:S(2)}) copy-start(bf16[1,512,2048]{2,1,0:T(8,128)(2,1)} %param.15) | copy-start | bytes 6291460
  7.2 11.3 %copy-start.2 = (s32[1,4]{1,0:T(1,128)S(1)}, s32[1,4]{1,0:T(1,128)}, u32[]{:S(2)}) copy-start(s32[1,4]{1,0:T(1,128)} %param.17) | copy-start | bytes 52
  7.2 12.0 %copy-start.3 = (s32[1,4]{1,0:T(1,128)S(1)}, s32[1,4]{1,0:T(1,128)}, u32[]{:S(2)}) copy-start(s32[1,4]{1,0:T(1,128)} %param.16) | copy-start | bytes 52
  7.2 124.5 %all-gather.2.cloned.1.call-start = ((), (), s32[]{:S(2)}) async-start(), calls=%async_computation.1 | async-start | bytes 4259840 | tf_op jit(solution)/shard_map/all_gather | solution.py:110
  7.9 332.5 %reduce-scatter.2.cloned.1.call-start = ((), (), s32[]{:S(2)}) async-start(), calls=%async_computation.2 | async-start | bytes 8519680 | tf_op jit(solution)/shard_map/reduce_scatter | solution.py:141
  10.6 1.3 copy-start.5
  13.4 14.9 %collective-permute-start.1 = (bf16[2,256,1024]{2,1,0:T(8,128)(2,1)}, bf16[2,256,1024]{2,1,0:T(8,128)(2,1)}, u32[]{:S(2)}, u32[]{:S(2)}) collective-permute-start(bf16[2,256,1024]{2,1,0:T(8,128)(2,1)} %get-tuple-element.91), channel_id=1, source_target_pairs={{4,0},{8,4},{12,8},{16,12},{20,16},{24,20},{28,24},{32,28},{36,32}... | collective-permute-start | bytes 3145736 | tf_op jit(solution)/shard_map/ppermute | solution.py:21
  15.3 17.4 %collective-permute-start = (bf16[2,256,1024]{2,1,0:T(8,128)(2,1)}, bf16[2,256,1024]{2,1,0:T(8,128)(2,1)}, u32[]{:S(2)}, u32[]{:S(2)}) collective-permute-start(bf16[2,256,1024]{2,1,0:T(8,128)(2,1)} %get-tuple-element.90), channel_id=1, source_target_pairs={{0,4},{4,8},{8,12},{12,16},{16,20},{20,24},{24,28},{28,32},{32,36}... | collective-permute-start | bytes 3145736 | tf_op jit(solution)/shard_map/ppermute | solution.py:18
  78.2 13.3 %copy-start.6 = (bf16[4,128,8,128]{1,3,2,0:T(8,128)(2,1)S(1)}, bf16[4,128,8,128]{1,3,2,0:T(8,128)(2,1)}, u32[]{:S(2)}) copy-start(bf16[4,128,8,128]{1,3,2,0:T(8,128)(2,1)} %copy.42) | copy-start | bytes 3145732
  123.1 273.8 %all-reduce.2.cloned.1.call-start = ((), (), s32[]{:S(2)}) async-start(), calls=%async_computation.3 | async-start | bytes 131072 | tf_op jit(solution)/shard_map/psum | solution.py:149
  296.9 38.9 %collective-permute-start.2 = (bf16[2,256,1024]{2,1,0:T(8,128)(2,1)}, bf16[2,256,1024]{2,1,0:T(8,128)(2,1)}, u32[]{:S(2)}, u32[]{:S(2)}) collective-permute-start(bf16[2,256,1024]{2,1,0:T(8,128)(2,1)} %get-tuple-element.87), channel_id=1, source_target_pairs={{0,4},{4,8},{8,12},{12,16},{16,20},{20,24},{24,28},{28,32},{32,36}... | collective-permute-start | bytes 3145736 | tf_op jit(solution)/shard_map/ppermute | solution.py:29
  298.8 39.3 %collective-permute-start.3 = (bf16[2,256,1024]{2,1,0:T(8,128)(2,1)}, bf16[2,256,1024]{2,1,0:T(8,128)(2,1)S(1)}, u32[]{:S(2)}, u32[]{:S(2)}) collective-permute-start(bf16[2,256,1024]{2,1,0:T(8,128)(2,1)} %get-tuple-element.86), channel_id=1, source_target_pairs={{4,0},{8,4},{12,8},{16,12},{20,16},{24,20},{28,24},{32,28},{36,32}... | collective-permute-start | bytes 3145736 | tf_op jit(solution)/shard_map/ppermute | solution.py:29
  321.9 7.9 %copy-start.7 = (bf16[4,128,8,128]{3,2,1,0:T(8,128)(2,1)S(1)}, bf16[4,128,8,128]{3,2,1,0:T(8,128)(2,1)}, u32[]{:S(2)}) copy-start(bf16[4,128,8,128]{3,2,1,0:T(8,128)(2,1)} %copy.34) | copy-start | bytes 3145732
  329.8 6.0 %copy-start.4 = (f32[2,512,1024]{2,1,0:T(8,128)S(1)}, f32[2,512,1024]{2,1,0:T(8,128)}, u32[]{:S(2)}) copy-start(f32[2,512,1024]{2,1,0:T(8,128)} %slice.163) | copy-start | bytes 12582916
  335.8 62.6 %copy-start.1 = (bf16[1,512,2048]{2,1,0:T(8,128)(2,1)S(1)}, bf16[1,512,2048]{2,1,0:T(8,128)(2,1)}, u32[]{:S(2)}) copy-start(bf16[1,512,2048]{2,1,0:T(8,128)(2,1)} %param.15) | copy-start | bytes 6291460
Sparse Core Ops, SparseCore 0:
  10.8 80.8 all-gather.1
  123.3 156.2 reduce-scatter.1
  342.1 54.7 all-reduce.1
where the time goes:
time: 408 us; the launch traced here: 405 us
  local copies, waits for them, and re-layouts  168 us (41%)
  matrix products  96.1 us (24%)
  waiting for transfers between devices  62.5 us (15%)
  other arithmetic  46.3 us (11%)
  between operations  21.7 us (5%)
  starting transfers between devices  10.2 us (2%)
    dynamic_update_slice x4, local copies, waits for them, and re-layouts, advance(): lax.dynamic_update_slice_in_dim(running, current + contributions[member],...  59.1 us
    psum x1, waiting for transfers between devices, body(): summed = lax.psum(shard_sum.astype(jnp.bfloat16), 'dp').astype(jnp.float32)  51.9 us
    add x3, other arithmetic, advance(): current + contributions[member]  25.1 us
    reshape x2, local copies, waits for them, and re-layouts, advance(): contributions = jnp.stack([key_part, value_part], axis=1)  22.8 us
    gather x12, local copies, waits for them, and re-layouts  20.9 us
    dot_general x1, matrix products, advance(): jnp.einsum('jhqk,jkhd->jqhd', grad_scores, key_tiles, preferred_element_t...  19.4 us
    dot_general x1, matrix products, advance(): jnp.einsum('jhqk,jqhd->jkhd', grad_scores, query_set, preferred_element_t...  18.9 us
    gather x1, local copies, waits for them, and re-layouts, advance(): lax.dynamic_slice_in_dim(kv_source, offset, window_rows, 1)  15.4 us
  transfers between devices with their start and end apart: 7, of which 3 were waited for; matrix products, arithmetic and copies ran while one was open for 76% of the time, Pallas kernels for 0%

commit v1 on v0

--- a/solution.py
+++ b/solution.py
@@ -146,7 +146,9 @@
         scatter_dimension=0,
         tiled=True,
     )
-    summed = lax.psum(shard_sum.astype(jnp.bfloat16), "dp").astype(jnp.float32)
+    summed = jnp.sum(jax.lax.all_gather(shard_sum.astype(jnp.bfloat16), "dp"), axis=0).astype(
+        jnp.float32
+    )
     weight_grad = summed / normalizer
     return (layer_out[None], grad_query[None], key_grad[None], value_grad[None], weight_grad)
 

time: 408 us -> 374 us (0.917)
  the two profiles are of different devices: /device:TPU:8 before, /device:TPU:128 now
where the time goes in v1:
time: 374 us; the launch traced here: 370 us
  local copies, waits for them, and re-layouts  166 us (44%)
  matrix products  96.3 us (26%)
  other arithmetic  43.3 us (12%)
  between operations  22 us (6%)
  starting transfers between devices  14.8 us (4%)
  waiting for transfers between devices  14.6 us (4%)
  blocking collectives  12.9 us (3%)
    dynamic_update_slice x4, local copies, waits for them, and re-layouts, advance(): lax.dynamic_update_slice_in_dim(running, current + contributions[member],...  59 us
    add x3, other arithmetic, advance(): current + contributions[member]  24.9 us
    reshape x2, local copies, waits for them, and re-layouts, advance(): contributions = jnp.stack([key_part, value_part], axis=1)  22.9 us
    gather x12, local copies, waits for them, and re-layouts  21 us
    dot_general x1, matrix products, advance(): jnp.einsum('jhqk,jkhd->jqhd', grad_scores, key_tiles, preferred_element_t...  19.5 us
    dot_general x1, matrix products, advance(): jnp.einsum('jhqk,jqhd->jkhd', grad_scores, query_set, preferred_element_t...  19 us
    gather x1, local copies, waits for them, and re-layouts, advance(): lax.dynamic_slice_in_dim(kv_source, offset, window_rows, 1)  15 us
    sub x1, matrix products, advance(): raised = jnp.where(inside, jnp.exp(scores - highest), 0.0)  14 us
  transfers between devices with their start and end apart: 6, of which 2 were waited for; matrix products, arithmetic and copies ran while one was open for 82% of the time, Pallas kernels for 0%

profile of v1, /device:TPU:128, one launch (start us, length us, event | category | flops | bytes accessed | tf_op | source)
XLA Modules:
  0.0 370.2 jit_solution(17527883388978645644)
XLA Ops:
  24.4 6.1 %collective-permute-done.1 = bf16[2,256,1024]{2,1,0:T(8,128)(2,1)} collective-permute-done((bf16[2,256,1024]{2,1,0:T(8,128)(2,1)}, bf16[2,256,1024]{2,1,0:T(8,128)(2,1)}, u32[]{:S(2)}, u32[]{:S(2)}) %collective-permute-start.1) | collective-permute-done | bytes 1048608 | tf_op jit(solution)/shard_map/ppermute | solution.py:21
  30.4 7.8 %collective-permute-done = bf16[2,256,1024]{2,1,0:T(8,128)(2,1)} collective-permute-done((bf16[2,256,1024]{2,1,0:T(8,128)(2,1)}, bf16[2,256,1024]{2,1,0:T(8,128)(2,1)}, u32[]{:S(2)}, u32[]{:S(2)}) %collective-permute-start) | collective-permute-done | bytes 1048608 | tf_op jit(solution)/shard_map/ppermute | solution.py:18
  42.0 21.0 %while.3 = (s32[]{:T(128)}, bf16[2,1024,1024]{2,1,0:T(8,128)(2,1)}, s32[4,3]{1,0:T(4,128)S(1)}, bf16[4,2,640,1024]{3,2,1,0:T(8,128)(2,1)}, s32[]{:T(128)}) while((s32[]{:T(128)}, bf16[2,1024,1024]{2,1,0:T(8,128)(2,1)}, s32[4,3]{1,0:T(4,128)S(1)}, bf16[4,2,640,1024]{3,2,1,0:T(8,128)(2,1)}, s32[]{:T(128)}) %tuple.39), condition=%wide.while_cond.2, body=%wide.while_body.2.sunk | while | flops 2 | bytes 5243501 | solution.py:45
  68.5 15.0 %copy.30 = bf16[4,2,640,1024]{2,3,0,1:T(8,128)(2,1)} copy(bf16[4,2,640,1024]{3,2,1,0:T(8,128)(2,1)} %get-tuple-element.69) | data formatting | bytes 20971520 | tf_op jit(solution)/shard_map/while/body/eval_jaxpr/vmap()/gather | solution.py:45
  83.4 8.0 %copy.29 = bf16[4,1,640,1024]{2,3,0,1:T(8,128)(2,1)} copy(bf16[4,1,640,1024]{3,2,1,0:T(8,128)(2,1)} %slice.116) | data formatting | bytes 10485760 | tf_op jit(solution)/shard_map/while/body/eval_jaxpr/slice | solution.py:48
  96.8 14.0 %bitcast_reduce_fusion = (f32[4,8,128]{2,1,0:T(8,128)S(1)}, f32[4,8,640,128]{3,2,1,0:T(8,128)}) fusion(pred[4,640]{1,0:T(4,128)(4,1)S(1)} %compare_and_fusion, bf16[4,640,8,128]{1,3,2,0:T(8,128)(2,1)} %bitcast.113, bf16[4,128,8,128]{1,3,2,0:T(8,128)(2,1)S(1)} %copy-done.6), kind=kOutput, calls=%fused_computation.14 | convolution fusion | flops 1357906560 | bytes 16796160 | tf_op jit(solution)/shard_map/while/body/eval_jaxpr/sub | solution.py:61
  110.8 8.0 %fusion.50 = bf16[4,128,8,128]{1,3,2,0:T(8,128)(2,1)} fusion(bf16[4,640,8,128]{1,3,2,0:T(8,128)(2,1)} %bitcast.109, f32[4,8,640,128]{3,2,1,0:T(8,128)} %get-tuple-element.97, f32[4,8,128]{2,1,0:T(8,128)S(1)} %get-tuple-element.96), kind=kOutput, calls=%fused_computation.58 | convolution fusion | flops 676855808 | bytes 16793600 | tf_op jit(solution)/shard_map/while/body/eval_jaxpr/jhqk,jkhd->jqhd/dot_general | solution.py:64
  121.2 7.0 %fusion.37 = f32[1024,2048]{1,0:T(8,128)} fusion(bf16[1,512,2048]{2,1,0:T(8,128)(2,1)S(1)} %copy-done, bf16[64,8,8,128]{3,2,1,0:T(8,128)(2,1)} %bitcast.119), kind=kOutput, calls=%fused_computation.51 | convolution fusion | flops 2147483648 | bytes 11534336 | tf_op jit(solution)/shard_map/dot_general | solution.py:142
  142.3 8.0 %fusion.78 = f32[4,8,128,640]{2,3,1,0:T(8,128)} fusion(bf16[4,128,8,128]{1,3,2,0:T(8,128)(2,1)S(1)} %copy.43, bf16[4,640,8,128]{1,3,2,0:T(8,128)(2,1)} %bitcast.110), kind=kOutput, calls=%fused_computation.94 | convolution fusion | flops 671088640 | bytes 16777216 | tf_op jit(solution)/shard_map/while/body/eval_jaxpr/jqhd,jkhd->jhqk/dot_general | solution.py:67
  150.3 19.0 %fusion.10 = f32[4,8,640,128]{2,3,1,0:T(8,128)} fusion(bf16[4,128,8,128]{1,3,2,0:T(8,128)(2,1)S(1)} %copy-done.6, f32[4,8,128,640]{2,3,1,0:T(8,128)} %fusion.78, f32[4,8,640,128]{3,2,1,0:T(8,128)} %get-tuple-element.97, f32[4,8,128]{2,1,0:T(8,128)S(1)} %get-tuple-element.96), kind=kOutput, calls=%fused_computation.22 | convolution fusion | flops 689443456 | bytes 32522240 | tf_op jit(solution)/shard_map/while/body/eval_jaxpr/jhqk,jqhd->jkhd/dot_general | solution.py:75
  169.3 11.5 %copy.45 = f32[4,1,640,1024]{3,2,1,0:T(8,128)} copy(f32[4,1,640,1024]{2,3,0,1:T(8,128)} %bitcast.111) | data formatting | bytes 20971520 | tf_op jit(solution)/shard_map/while/body/eval_jaxpr/stack;while/body/eval_jaxpr/reshape | solution.py:81
  180.9 10.2 %fusion.31 = f32[4,8,128,640]{3,2,1,0:T(8,128)} fusion(bf16[4,128,8,128]{1,3,2,0:T(8,128)(2,1)S(1)} %copy.43, f32[4,8,640,128]{3,2,1,0:T(8,128)} %get-tuple-element.97, f32[4,8,128]{2,1,0:T(8,128)S(1)} %get-tuple-element.96), kind=kOutput, calls=%fused_computation.43 | convolution fusion | flops 676331520 | bytes 22036480 | tf_op jit(solution)/shard_map/while/body/eval_jaxpr/jhqk,jqhd->jkhd/dot_general | solution.py:78
  191.0 11.3 %copy.46 = f32[4,1,640,1024]{3,2,1,0:T(8,128)} copy(f32[4,1,640,1024]{2,3,0,1:T(8,128)} %bitcast.112) | data formatting | bytes 20971520 | tf_op jit(solution)/shard_map/while/body/eval_jaxpr/stack;while/body/eval_jaxpr/reshape | solution.py:81
  212.3 15.0 %dynamic_update_slice.21 = f32[2,1024,1024]{2,1,0:T(8,128)} dynamic-update-slice(f32[2,1024,1024]{2,1,0:T(8,128)} %broadcast_in_dim.65, f32[2,640,1024]{2,1,0:T(8,128)} %fusion.19, s32[]{:T(128)} %constant.107.clone.1, s32[]{:T(128)S(6)} %select_n.64, s32[]{:T(128)} %constant.107.clone.1) | dynamic-update-slice | bytes 10485764 | tf_op jit(solution)/shard_map/while/body/eval_jaxpr/dynamic_update_slice | solution.py:85
  227.3 8.3 %fusion.22 = f32[2,640,1024]{2,1,0:T(8,128)} fusion(f32[4,1,640,1024]{3,2,1,0:T(8,128)} %copy.45, f32[4,1,640,1024]{3,2,1,0:T(8,128)} %copy.46, f32[2,1024,1024]{2,1,0:T(8,128)} %dynamic_update_slice.21, s32[]{:T(128)S(6)} %select_n.65), kind=kLoop, calls=%fused_computation.31 | loop fusion | flops 2621440 | bytes 31457284 | tf_op jit(solution)/shard_map/while/body/eval_jaxpr/add | solution.py:86
  235.6 14.9 %dynamic_update_slice.22 = f32[2,1024,1024]{2,1,0:T(8,128)} dynamic-update-slice(f32[2,1024,1024]{2,1,0:T(8,128)} %dynamic_update_slice.21, f32[2,640,1024]{2,1,0:T(8,128)} %fusion.22, s32[]{:T(128)} %constant.107.clone.1, s32[]{:T(128)S(6)} %select_n.65, s32[]{:T(128)} %constant.107.clone.1) | dynamic-update-slice | bytes 10485764 | tf_op jit(solution)/shard_map/while/body/eval_jaxpr/dynamic_update_slice | solution.py:85
  250.5 8.3 %fusion.17 = f32[2,640,1024]{2,1,0:T(8,128)} fusion(f32[4,1,640,1024]{3,2,1,0:T(8,128)} %copy.45, f32[4,1,640,1024]{3,2,1,0:T(8,128)} %copy.46, f32[2,1024,1024]{2,1,0:T(8,128)} %dynamic_update_slice.22, s32[]{:T(128)S(6)} %select_n.66), kind=kLoop, calls=%fused_computation.26 | loop fusion | flops 2621440 | bytes 31457284 | tf_op jit(solution)/shard_map/while/body/eval_jaxpr/add | solution.py:86
  258.8 14.9 %dynamic_update_slice.23 = f32[2,1024,1024]{2,1,0:T(8,128)} dynamic-update-slice(f32[2,1024,1024]{2,1,0:T(8,128)} %dynamic_update_slice.22, f32[2,640,1024]{2,1,0:T(8,128)} %fusion.17, s32[]{:T(128)} %constant.107.clone.1, s32[]{:T(128)S(6)} %select_n.66, s32[]{:T(128)} %constant.107.clone.1) | dynamic-update-slice | bytes 10485764 | tf_op jit(solution)/shard_map/while/body/eval_jaxpr/dynamic_update_slice | solution.py:85
  273.7 8.3 %fusion.24 = f32[2,640,1024]{2,1,0:T(8,128)} fusion(f32[4,1,640,1024]{3,2,1,0:T(8,128)} %copy.46, f32[4,1,640,1024]{3,2,1,0:T(8,128)} %copy.45, f32[2,1024,1024]{2,1,0:T(8,128)} %dynamic_update_slice.23, s32[]{:T(128)S(6)} %select_n.67), kind=kLoop, calls=%fused_computation.34 | loop fusion | flops 2621440 | bytes 31457284 | tf_op jit(solution)/shard_map/while/body/eval_jaxpr/add | solution.py:86
  282.0 14.3 %dynamic_update_slice.24 = f32[2,1024,1024]{2,1,0:T(8,128)} dynamic-update-slice(f32[2,1024,1024]{2,1,0:T(8,128)} %dynamic_update_slice.23, f32[2,640,1024]{2,1,0:T(8,128)} %fusion.24, s32[]{:T(128)} %constant.107.clone.1, s32[]{:T(128)S(6)} %select_n.67, s32[]{:T(128)} %constant.107.clone.1) | dynamic-update-slice | bytes 10485764 | tf_op jit(solution)/shard_map/while/body/eval_jaxpr/dynamic_update_slice | solution.py:85
  303.7 7.0 %collective-permute-start.3 = (bf16[2,256,1024]{2,1,0:T(8,128)(2,1)}, bf16[2,256,1024]{2,1,0:T(8,128)(2,1)S(1)}, u32[]{:S(2)}, u32[]{:S(2)}) collective-permute-start(bf16[2,256,1024]{2,1,0:T(8,128)(2,1)} %get-tuple-element.86), channel_id=1, source_target_pairs={{4,0},{8,4},{12,8},{16,12},{20,16},{24,20},{28,24},{32,28},{36,32}... | collective-permute-start | bytes 3145736 | tf_op jit(solution)/shard_map/ppermute | solution.py:29
  310.7 19.5 %fusion.53 = bf16[4,128,8,128]{1,3,2,0:T(8,128)(2,1)} fusion(bf16[4,640,8,128]{1,3,2,0:T(8,128)(2,1)} %bitcast.114, f32[4,8,128,640]{2,3,1,0:T(8,128)} %fusion.78, f32[4,8,640,128]{3,2,1,0:T(8,128)} %get-tuple-element.97, f32[4,8,128]{2,1,0:T(8,128)S(1)} %get-tuple-element.96), kind=kOutput, calls=%fused_computation.59 | convolution fusion | flops 689967744 | bytes 27279360 | tf_op jit(solution)/shard_map/while/body/eval_jaxpr/jhqk,jkhd->jqhd/dot_general | solution.py:72
  338.1 6.0 %fusion.30 = bf16[1,512,2048]{2,1,0:T(8,128)(2,1)} fusion(bf16[1024,2048]{1,0:T(8,128)(2,1)} %all-gather.3.cloned.1.call-done, bf16[64,8,8,128]{3,2,1,0:T(8,128)(2,1)S(1)} %bitcast.120), kind=kOutput, calls=%fused_computation.42 | convolution fusion | flops 2148532224 | bytes 7340032 | tf_op jit(solution)/shard_map/dot_general | solution.py:137
  349.7 12.9 %all-gather = bf16[64,2048]{1,0:T(8,128)(2,1)S(1)} all-gather(bf16[16,2048]{1,0:T(8,128)(2,1)S(1)} %convert_element_type.58), channel_id=2, replica_groups=mesh['seq'=64,'dp'=4] {'dp'}, dimensions={0}, use_global_device_ids=true | all-gather | bytes 327680 | tf_op jit(solution)/shard_map/all_gather | solution.py:149
  (79 shorter events, 92.9 us)
Async XLA Ops:
  7.2 114.1 %copy-start = (bf16[1,512,2048]{2,1,0:T(8,128)(2,1)S(1)}, bf16[1,512,2048]{2,1,0:T(8,128)(2,1)}, u32[]{:S(2)}) copy-start(bf16[1,512,2048]{2,1,0:T(8,128)(2,1)} %param.15) | copy-start | bytes 6291460
  7.2 12.8 %copy-start.2 = (s32[1,4]{1,0:T(1,128)S(1)}, s32[1,4]{1,0:T(1,128)}, u32[]{:S(2)}) copy-start(s32[1,4]{1,0:T(1,128)} %param.17) | copy-start | bytes 52
  7.2 13.5 %copy-start.3 = (s32[1,4]{1,0:T(1,128)S(1)}, s32[1,4]{1,0:T(1,128)}, u32[]{:S(2)}) copy-start(s32[1,4]{1,0:T(1,128)} %param.16) | copy-start | bytes 52
  7.2 129.4 %all-gather.3.cloned.1.call-start = ((), (), s32[]{:S(2)}) async-start(), calls=%async_computation.1 | async-start | bytes 4259840 | tf_op jit(solution)/shard_map/all_gather | solution.py:110
  7.9 340.9 %reduce-scatter.2.cloned.1.call-start = ((), (), s32[]{:S(2)}) async-start(), calls=%async_computation.2 | async-start | bytes 8519680 | tf_op jit(solution)/shard_map/reduce_scatter | solution.py:141
  10.6 1.3 copy-start.5
  13.4 17.0 %collective-permute-start.1 = (bf16[2,256,1024]{2,1,0:T(8,128)(2,1)}, bf16[2,256,1024]{2,1,0:T(8,128)(2,1)}, u32[]{:S(2)}, u32[]{:S(2)}) collective-permute-start(bf16[2,256,1024]{2,1,0:T(8,128)(2,1)} %get-tuple-element.91), channel_id=1, source_target_pairs={{4,0},{8,4},{12,8},{16,12},{20,16},{24,20},{28,24},{32,28},{36,32}... | collective-permute-start | bytes 3145736 | tf_op jit(solution)/shard_map/ppermute | solution.py:21
  17.3 20.9 %collective-permute-start = (bf16[2,256,1024]{2,1,0:T(8,128)(2,1)}, bf16[2,256,1024]{2,1,0:T(8,128)(2,1)}, u32[]{:S(2)}, u32[]{:S(2)}) collective-permute-start(bf16[2,256,1024]{2,1,0:T(8,128)(2,1)} %get-tuple-element.90), channel_id=1, source_target_pairs={{0,4},{4,8},{8,12},{12,16},{16,20},{20,24},{24,28},{28,32},{32,36}... | collective-permute-start | bytes 3145736 | tf_op jit(solution)/shard_map/ppermute | solution.py:18
  83.4 13.3 %copy-start.6 = (bf16[4,128,8,128]{1,3,2,0:T(8,128)(2,1)S(1)}, bf16[4,128,8,128]{1,3,2,0:T(8,128)(2,1)}, u32[]{:S(2)}) copy-start(bf16[4,128,8,128]{1,3,2,0:T(8,128)(2,1)} %copy.42) | copy-start | bytes 3145732
  301.8 42.2 %collective-permute-start.2 = (bf16[2,256,1024]{2,1,0:T(8,128)(2,1)}, bf16[2,256,1024]{2,1,0:T(8,128)(2,1)}, u32[]{:S(2)}, u32[]{:S(2)}) collective-permute-start(bf16[2,256,1024]{2,1,0:T(8,128)(2,1)} %get-tuple-element.87), channel_id=1, source_target_pairs={{0,4},{4,8},{8,12},{12,16},{16,20},{20,24},{24,28},{28,32},{32,36}... | collective-permute-start | bytes 3145736 | tf_op jit(solution)/shard_map/ppermute | solution.py:29
  303.7 42.6 %collective-permute-start.3 = (bf16[2,256,1024]{2,1,0:T(8,128)(2,1)}, bf16[2,256,1024]{2,1,0:T(8,128)(2,1)S(1)}, u32[]{:S(2)}, u32[]{:S(2)}) collective-permute-start(bf16[2,256,1024]{2,1,0:T(8,128)(2,1)} %get-tuple-element.86), channel_id=1, source_target_pairs={{4,0},{8,4},{12,8},{16,12},{20,16},{24,20},{28,24},{32,28},{36,32}... | collective-permute-start | bytes 3145736 | tf_op jit(solution)/shard_map/ppermute | solution.py:29
  330.2 7.9 %copy-start.7 = (bf16[4,128,8,128]{3,2,1,0:T(8,128)(2,1)S(1)}, bf16[4,128,8,128]{3,2,1,0:T(8,128)(2,1)}, u32[]{:S(2)}) copy-start(bf16[4,128,8,128]{3,2,1,0:T(8,128)(2,1)} %copy.34) | copy-start | bytes 3145732
  338.0 6.0 %copy-start.4 = (f32[2,512,1024]{2,1,0:T(8,128)S(1)}, f32[2,512,1024]{2,1,0:T(8,128)}, u32[]{:S(2)}) copy-start(f32[2,512,1024]{2,1,0:T(8,128)} %slice.163) | copy-start | bytes 12582916
  344.1 19.3 %copy-start.1 = (bf16[1,512,2048]{2,1,0:T(8,128)(2,1)S(1)}, bf16[1,512,2048]{2,1,0:T(8,128)(2,1)}, u32[]{:S(2)}) copy-start(bf16[1,512,2048]{2,1,0:T(8,128)(2,1)} %param.15) | copy-start | bytes 6291460
Sparse Core Ops, SparseCore 0:
  10.8 78.0 all-gather.2
  128.3 148.9 reduce-scatter.1
